TPU v7x, 32 devices: a whole 2x2x4 slice. The times are simulated.
32 devices in a mesh: groups: 2 (over x), seq: 16 (over z, y, core).
Axes of the slice: x: 2, y: 2, z: 4, core: 2. Of those that a mesh axis runs over, the one named last changes fastest.
Arguments:
- queries: bfloat16 [96, 8192], P(('groups', 'seq')), parts along dimension 0, may hold values from -48 to 48
- prompt_of: int32 [96, 1], P(('groups', 'seq')), parts along dimension 0, may hold values from 0 to 1; in each aligned block of 3 rows (0 to 2, 3 to 5, ...) at most 2 rows name the same one
- suffix_cache: bfloat16 [96, 512, 2048], P(('groups', 'seq')), parts along dimension 0, may hold values from -6 to 6
- suffix_blocks: int32 [96], P(('groups', 'seq')), parts along dimension 0, may hold values from 1 to 4
- prompt_cache: bfloat16 [4, 2048, 2048], P('groups', 'seq'), parts along dimension 0, may hold values from -16 to 16
- reward_weight: float32 [8192], replicated, may hold values from -0.4375 to 0.4375
Outputs:
- attended: bfloat16 [96, 8192], P(('groups', 'seq')), parts along dimension 0
- scores: float32 [96], P(('groups', 'seq')), parts along dimension 0
There are 2 independent parts, one for each index of `groups`. A program takes and returns all parts, laid end to end along the dimension named above; an argument that names none is the same for every part. Nothing has to cross between parts.
Inputs may be any that keep to these rules, and one draw needn't show every extreme that they name: `prompt_of`: in each device's aligned block of 3 rows at most 2 candidates name the same prompt.
All inputs are finite; a program needn't handle non-finite values.
Results may differ from a plain program's by a relative error of at most 0.015.
Values may be sent and summed in bfloat16 or wider, within the bound.
A program may use at most 192 MiB of HBM per device.

v0:
```python
import math

import jax
import jax.numpy as jnp
from jax import lax
from jax.sharding import PartitionSpec as P

HD = 128
CAP = 2
BLOCK = 128


floor_logit = -1e30


def attend_block(query_rows, keys, values):
    row_count = query_rows.shape[0]
    kv_heads = keys.shape[1]
    head_dim = keys.shape[2]
    grouped = query_rows.reshape(row_count, kv_heads, -1, head_dim)
    logits = jnp.einsum(
        "nkgd,tkd->nkgt", grouped, keys, preferred_element_type=jnp.float32
    ) * head_dim ** (-0.5)
    maxima = jnp.max(logits, axis=-1)
    exponent = jnp.exp(logits - maxima[..., None])
    totals = jnp.sum(exponent, axis=-1)
    weights = exponent.astype(jnp.bfloat16)
    weighted = jnp.einsum("nkgt,tkd->nkgd", weights, values, preferred_element_type=jnp.float32)
    return (
        maxima.reshape(row_count, -1),
        totals.reshape(row_count, -1),
        weighted.reshape(row_count, -1),
    )


def body(queries, prompt_of, suffix_cache, suffix_blocks, prompt_cache, reward_weight):
    cand_rows = queries.shape[0]
    prompts = prompt_cache.shape[0]
    prompt_span = prompt_cache.shape[1]
    kv_width = prompt_cache.shape[2] // 2
    kv_heads = kv_width // HD
    heads = queries.shape[1] // HD
    keys_local = prompt_cache[:, :, :kv_width].reshape(prompts, prompt_span, kv_heads, HD)
    values_local = prompt_cache[:, :, kv_width:].reshape(prompts, prompt_span, kv_heads, HD)
    suffix_len = suffix_cache.shape[1]
    suffix_keys = suffix_cache[:, :, :kv_width].reshape(cand_rows, suffix_len, kv_heads, HD)
    suffix_values = suffix_cache[:, :, kv_width:].reshape(cand_rows, suffix_len, kv_heads, HD)
    grouped = queries.reshape(cand_rows, kv_heads, -1, HD)
    logits = jnp.einsum(
        "ckgd,ctkd->ckgt", grouped, suffix_keys, preferred_element_type=jnp.float32
    ) * HD ** (-0.5)
    live_mask = (jnp.arange(suffix_len)[None, :] < BLOCK * suffix_blocks[:, None])[:, None, None, :]
    logits = jnp.where(live_mask, logits, floor_logit)
    maxima = jnp.max(logits, axis=-1)
    exponent = jnp.where(live_mask, jnp.exp(logits - maxima[..., None]), 0.0)
    totals = jnp.sum(exponent, axis=-1)
    weighted = jnp.einsum(
        "ckgt,ctkd->ckgd",
        exponent.astype(jnp.bfloat16),
        suffix_values,
        preferred_element_type=jnp.float32,
    )
    suffix_state = (
        maxima.reshape(cand_rows, -1),
        totals.reshape(cand_rows, -1),
        weighted.reshape(cand_rows, -1),
    )
    prompt_ids = prompt_of[:, 0]
    prompt_hot = (prompt_ids[:, None] == jnp.arange(prompts)[None, :]).astype(jnp.float32)
    spread = 1
    earlier = (jnp.arange(cand_rows)[:, None] > jnp.arange(cand_rows)[None, :]).astype(jnp.float32)
    slot_rank = jnp.sum(jnp.dot(earlier, prompt_hot) * prompt_hot, axis=1).astype(jnp.int32)
    slot_index = prompt_ids * CAP + slot_rank
    slot_hot = (slot_index[:, None] == jnp.arange(prompts * CAP)[None, :]).astype(jnp.float32)
    row_block = jnp.einsum(
        "cs,cf->sf", slot_hot.astype(jnp.bfloat16), queries, preferred_element_type=jnp.float32
    ).astype(jnp.bfloat16)
    home_state = tuple(
        (
            jnp.einsum("cs,cf->sf", slot_hot, member, precision=lax.Precision.HIGHEST)
            for member in suffix_state
        )
    )

    def attend_rows(query_rows):
        shards = query_rows.shape[0] // (prompts * CAP)
        shaped = query_rows.reshape(shards, prompts, CAP, -1)
        parts_all = [
            attend_block(
                shaped[:, prompt].reshape(shards * CAP, -1),
                keys_local[prompt],
                values_local[prompt],
            )
            for prompt in range(prompts)
        ]
        return tuple(
            (
                jnp.stack(
                    [
                        parts_all[prompt][member].reshape(shards, CAP, -1)
                        for prompt in range(prompts)
                    ],
                    axis=1,
                ).reshape(shards * prompts * CAP, -1)
                for member in range(3)
            )
        )

    rows_dev = row_block.shape[0]
    width_heads = heads * spread
    devices = lax.axis_size("seq")
    query_rows = (lax.all_gather(row_block, "seq", axis=0, tiled=True),)[0]
    shards = query_rows.shape[0] // rows_dev
    block_size = math.gcd(shards, 16)
    query_blocks = query_rows.reshape(shards // block_size, block_size * rows_dev, -1)
    mapped = lax.map(attend_rows, query_blocks)
    fresh_state = tuple((member.reshape(shards * rows_dev, -1) for member in mapped))
    computed = tuple((fresh_rows for fresh_rows in fresh_state))
    returned = (
        lax.all_to_all(computed[0], "seq", split_axis=0, concat_axis=0, tiled=True),
        lax.all_to_all(computed[1], "seq", split_axis=0, concat_axis=0, tiled=True),
        lax.all_to_all(computed[2], "seq", split_axis=0, concat_axis=0, tiled=True),
    )
    back_max = returned[0].reshape(devices, rows_dev, width_heads)
    back_sum = returned[1].reshape(devices, rows_dev, width_heads)
    back_mix = returned[2].reshape(devices, rows_dev, width_heads, HD)
    joined = jnp.maximum(jnp.max(back_max, axis=0), home_state[0])
    factor = jnp.exp(back_max - joined[None])
    home_factor = jnp.exp(home_state[0] - joined)
    totals_all = jnp.sum(factor * back_sum, axis=0) + home_factor * home_state[1]
    mixed_all = jnp.sum(factor[..., None] * back_mix, axis=0) + home_factor[..., None] * home_state[
        2
    ].reshape(rows_dev, width_heads, HD)
    final_state = (joined, totals_all, mixed_all.reshape(rows_dev, -1))
    out_rows = final_state[1].shape[0]
    attended_rows = (
        final_state[2].reshape(out_rows, heads, HD) / final_state[1][..., None]
    ).reshape(out_rows, -1)
    attended = jnp.einsum(
        "cs,sf->cf", slot_hot, attended_rows, precision=lax.Precision.HIGHEST
    ).astype(jnp.bfloat16)
    scores = jnp.sum(attended.astype(jnp.float32) * reward_weight, axis=-1)
    return (attended, scores)


def solution(mesh):
    placed = (
        P(("groups", "seq"), None),
        P(("groups", "seq"), None),
        P(("groups", "seq"), None, None),
        P(("groups", "seq")),
        P("groups", "seq", None),
        P(),
    )
    return jax.shard_map(
        body,
        mesh=mesh,
        in_specs=placed,
        out_specs=(P(("groups", "seq"), None), P(("groups", "seq"))),
        check_vma=False,
    )
```

profile of v0, /device:TPU:13, one launch (start us, length us, event | category | flops | bytes accessed | tf_op | source)
XLA Modules:
  0.0 144.3 jit_solution(13109195820663340520)
XLA Ops:
  7.2 0.9 fusion.8
  8.1 0.7 fusion.38
  8.7 0.5 copy-done.5
  9.2 1.6 %fusion = bf16[1,4,8192]{2,1,0:T(4,128)(2,1)} fusion(bf16[3,8192]{1,0:T(4,128)(2,1)} %param.6, s32[3]{0:T(128)S(1)} %fusion.38), kind=kOutput, calls=%fused_computation.2 | convolution fusion | flops 229412 | bytes 114700 | tf_op jit(solution)/shard_map/cs,cf->sf/dot_general | solution.py:75
  10.9 1.3 fusion.42
  12.1 0.2 copy.104
  12.3 0.2 copy.102
  12.5 0.9 copy.107
  13.4 0.9 copy.106
  14.2 35.1 %all-gather.3.cloned.1.call-done = bf16[16,4,8192]{2,1,0:T(4,128)(2,1)} async-done(((bf16[1,4,8192]{2,1,0:T(4,128)(2,1)}), bf16[16,4,8192]{2,1,0:T(4,128)(2,1)}) %all-gather.3.cloned.1.call-update) | async-done | bytes 1048592 | tf_op jit(solution)/shard_map/all_gather | solution.py:112
  49.3 2.8 %reshape.139 = bf16[16,2,2,8192]{3,2,1,0:T(2,128)(2,1)S(1)} reshape(bf16[16,4,8192]{2,1,0:T(4,128)(2,1)} %all-gather.3.cloned.1.call-done) | data formatting | bytes 2097152 | tf_op jit(solution)/shard_map/while/body/eval_jaxpr/reshape | solution.py:87
  52.0 1.2 slice_bitcast_fusion.1
  53.3 0.4 squeeze.30
  53.7 0.5 fusion.44
  54.2 0.1 copy.66
  54.3 0.7 fusion.11
  55.0 0.1 copy.83
  55.0 0.1 reshape.150
  55.1 0.4 squeeze.28
  55.5 0.5 fusion.45
  56.1 0.1 copy.61
  56.1 0.7 fusion.9
  56.8 0.1 copy.82
  56.9 0.1 reshape.149
  57.1 0.7 reshape.163
  57.8 5.2 %all-to-all-start.2 = ((f32[16,1,256]{2,1,0:T(1,128)}), f32[16,1,256]{2,1,0:T(1,128)S(1)}, u32[]{:S(2)}, u32[]{:S(2)}) async-start(f32[16,1,256]{2,1,0:T(1,128)} %reshape.163), calls=%async_computation.2 | async-start | bytes 32768 | tf_op jit(solution)/shard_map/all_to_all | solution.py:121
  62.9 0.1 reshape.141
  63.1 0.1 reshape.140
  63.2 1.4 convolution_bitcast_fusion
  64.6 1.4 convolution_bitcast_fusion.1
  66.0 0.7 reshape.161
  66.7 0.1 copy.76
  66.9 0.6 reshape.146
  67.5 0.1 copy.73
  67.6 0.6 reshape.145
  68.2 6.0 %all-to-all-start = ((f32[16,1,256]{2,1,0:T(1,128)}), f32[16,1,256]{2,1,0:T(1,128)S(1)}, u32[]{:S(2)}, u32[]{:S(2)}) async-start(f32[16,1,256]{2,1,0:T(1,128)} %reshape.161), calls=%async_computation | async-start | bytes 32768 | tf_op jit(solution)/shard_map/all_to_all | solution.py:120
  74.2 1.5 %pad_maximum_fusion = f32[16,2,2,8192]{3,2,0,1:T(2,128)S(1)} fusion(f32[16,1,2,8192]{3,2,0,1:T(2,128)S(1)} %reshape.146, f32[16,1,2,8192]{3,2,0,1:T(2,128)S(1)} %reshape.145), kind=kLoop, calls=%fused_computation.3 | loop fusion | flops 524288 | bytes 4194304 | tf_op jit(solution)/shard_map/while/body/eval_jaxpr/stack | solution.py:98
  75.8 1.2 copy.77
  77.0 2.7 %copy.78 = f32[16,4,8192]{2,1,0:T(4,128)} copy(f32[16,4,8192]{2,0,1:T(8,128)S(1)} %bitcast.93) | data formatting | bytes 4194304 | tf_op jit(solution)/shard_map/all_to_all | solution.py:122
  79.7 6.0 %all-to-all-start.1 = ((f32[16,4,8192]{2,1,0:T(4,128)}), f32[16,4,8192]{2,1,0:T(4,128)}, u32[]{:S(2)}, u32[]{:S(2)}) async-start(f32[16,4,8192]{2,1,0:T(4,128)} %copy.78), calls=%async_computation.1 | async-start | bytes 4194304 | tf_op jit(solution)/shard_map/all_to_all | solution.py:122
  85.7 5.6 %fusion.41 = (bf16[3,512,1024]{2,1,0:T(8,128)(2,1)}, bf16[3,512,1024]{2,1,0:T(8,128)(2,1)S(1)}) fusion(bf16[3,512,2048]{2,1,0:T(8,128)(2,1)} %param.8), kind=kLoop, calls=%fused_computation.68 | loop fusion | bytes 12582912 | tf_op jit(solution)/shard_map/slice | solution.py:46
  91.3 3.0 %copy.108 = bf16[3,512,1024]{1,2,0:T(8,128)(2,1)} copy(bf16[3,512,1024]{2,1,0:T(8,128)(2,1)S(1)} %get-tuple-element.28) | data formatting | bytes 6291456
  94.3 3.2 %copy.105 = bf16[3,512,1024]{1,2,0:T(8,128)(2,1)S(1)} copy(bf16[3,512,1024]{2,1,0:T(8,128)(2,1)} %get-tuple-element.20) | data formatting | bytes 6291456
  97.5 0.1 iota_compare_fusion
  97.6 1.4 fusion.43
  99.0 0.1 reshape.144
  99.1 0.2 fusion.19
  99.3 0.1 reshape.151
  99.4 2.8 %convolution_bitcast_fusion.2 = f32[1,3,64,128]{3,2,1,0:T(8,128)S(1)} fusion(bf16[3,512,8,128]{1,3,2,0:T(8,128)(2,1)} %bitcast.92, f32[3,8,8,512]{3,2,1,0:T(8,128)S(1)} %get-tuple-element.36, f32[3,8,8]{2,1,0:T(8,128)S(1)} %get-tuple-element.35, pred[3,512]{1,0:T(4,128)(4,1)S(1)} %iota_compare_fusion), kind=kOutput, calls=%fused_computation.17 | convolution fusion | flops 25460736 | bytes 3639552 | tf_op jit(solution)/shard_map/ckgt,ctkd->ckgd/dot_general | solution.py:57
  102.3 0.5 broadcast.48
  102.8 0.7 reduce.2
  103.5 0.1 reshape.164
  103.6 0.7 reduce.3
  104.3 0.1 reshape.162
  104.4 0.1 subtract_exponential_fusion.3
  104.6 2.0 %mul.73 = f32[16,4,64,128]{3,2,1,0:T(8,128)} broadcast(f32[16,4,64]{2,1,0:T(4,128)S(1)} %get-tuple-element.19), dimensions={0,1,2} | broadcast | bytes 2113536 | tf_op jit(solution)/shard_map/mul | solution.py:131
  106.5 2.1 %mul.74 = f32[16,4,8192]{2,1,0:T(4,128)S(1)} reshape(f32[16,4,64,128]{3,2,1,0:T(8,128)} %mul.73) | data formatting | bytes 4194304 | tf_op jit(solution)/shard_map/mul | solution.py:131
  108.6 0.1 copy.79
  108.7 0.1 fusion.7
  108.8 0.1 copy.86
  108.9 24.3 %all-to-all-done.1 = f32[16,4,8192]{2,1,0:T(4,128)} async-done(((f32[16,4,8192]{2,1,0:T(4,128)}), f32[16,4,8192]{2,1,0:T(4,128)}, u32[]{:S(2)}, u32[]{:S(2)}) %all-to-all-start.1) | async-done | bytes 2097184 | tf_op jit(solution)/shard_map/all_to_all | solution.py:122
  133.2 2.3 %multiply_reduce_fusion = f32[4,8192]{1,0:T(4,128)S(1)} fusion(f32[16,4,8192]{2,1,0:T(4,128)S(1)} %mul.74, f32[16,4,8192]{2,1,0:T(4,128)} %all-to-all-done.1), kind=kLoop, calls=%fused_computation.4 | loop fusion | flops 1015808 | bytes 4325376 | tf_op jit(solution)/shard_map/reduce_sum | solution.py:131
  135.5 0.3 fusion.6
  135.9 1.6 %multiply_reduce_fusion.1 = (f32[3]{0:T(128)}, bf16[3,8192]{1,0:T(4,128)(2,1)}) fusion(f32[8192]{0:T(1024)S(1)} %copy-done.4, f32[4,8192]{1,0:T(4,128)S(1)} %fusion.6, s32[3]{0:T(128)S(1)} %copy-done.6), kind=kOutput, calls=%fused_computation.42 | convolution fusion | flops 1277961 | bytes 213016 | tf_op jit(solution)/shard_map/cs,sf->cf/dot_general | solution.py:139
  (28 shorter events, 0.2 us)
Async XLA Ops:
  7.2 42.1 %all-gather.3.cloned.1.call-start = ((), (), s32[]{:S(2)}) async-start(), calls=%async_computation.3 | async-start | bytes 1114112 | tf_op jit(solution)/shard_map/all_gather | solution.py:112
  8.7 0.5 copy-start.5
  57.8 10.4 %all-to-all-start.2 = ((f32[16,1,256]{2,1,0:T(1,128)}), f32[16,1,256]{2,1,0:T(1,128)S(1)}, u32[]{:S(2)}, u32[]{:S(2)}) async-start(f32[16,1,256]{2,1,0:T(1,128)} %reshape.163), calls=%async_computation.2 | async-start | bytes 32768 | tf_op jit(solution)/shard_map/all_to_all | solution.py:121
  68.2 8.8 %copy-start = (f32[16,1,256]{2,1,0:T(1,128)}, f32[16,1,256]{2,1,0:T(1,128)S(1)}, u32[]{:S(2)}) copy-start(f32[16,1,256]{2,1,0:T(1,128)S(1)} %all-to-all-done.2) | copy-start | bytes 49156
  68.2 11.5 %all-to-all-start = ((f32[16,1,256]{2,1,0:T(1,128)}), f32[16,1,256]{2,1,0:T(1,128)S(1)}, u32[]{:S(2)}, u32[]{:S(2)}) async-start(f32[16,1,256]{2,1,0:T(1,128)} %reshape.161), calls=%async_computation | async-start | bytes 32768 | tf_op jit(solution)/shard_map/all_to_all | solution.py:120
  79.7 11.6 %copy-start.2 = (f32[16,1,256]{2,1,0:T(1,128)}, f32[16,1,256]{2,1,0:T(1,128)S(1)}, u32[]{:S(2)}) copy-start(f32[16,1,256]{2,1,0:T(1,128)S(1)} %all-to-all-done) | copy-start | bytes 49156
  79.7 53.5 %all-to-all-start.1 = ((f32[16,4,8192]{2,1,0:T(4,128)}), f32[16,4,8192]{2,1,0:T(4,128)}, u32[]{:S(2)}, u32[]{:S(2)}) async-start(f32[16,4,8192]{2,1,0:T(4,128)} %copy.78), calls=%async_computation.1 | async-start | bytes 4194304 | tf_op jit(solution)/shard_map/all_to_all | solution.py:122
  94.3 3.2 %copy-start.7 = (s32[3]{0:T(128)S(1)}, s32[3]{0:T(128)}, u32[]{:S(2)}) copy-start(s32[3]{0:T(128)} %param.9) | copy-start | bytes 40
  99.0 3.8 %copy-start.1 = (f32[16,1,256]{2,1,0:T(1,128)S(1)}, f32[16,1,256]{2,1,0:T(1,128)}, u32[]{:S(2)}) copy-start(f32[16,1,256]{2,1,0:T(1,128)} %copy-done) | copy-start | bytes 49156
  99.0 4.5 %copy-start.3 = (f32[16,1,256]{2,1,0:T(1,128)S(1)}, f32[16,1,256]{2,1,0:T(1,128)}, u32[]{:S(2)}) copy-start(f32[16,1,256]{2,1,0:T(1,128)} %copy-done.2) | copy-start | bytes 49156
  99.0 5.4 %copy-start.6 = (s32[3]{0:T(128)S(1)}, s32[3]{0:T(128)}, u32[]{:S(2)}) copy-start(s32[3]{0:T(128)} %copy-done.5) | copy-start | bytes 40
  108.6 27.2 %copy-start.4 = (f32[8192]{0:T(1024)S(1)}, f32[8192]{0:T(1024)}, u32[]{:S(2)}) copy-start(f32[8192]{0:T(1024)} %param.11) | copy-start | bytes 98308
Sparse Core Ops, SparseCore 0:
  11.0 38.2 all-gather.2
where the time goes:
time: 145 us; the launch traced here: 144 us
  waiting for transfers between devices  59.4 us (41%)
  local copies, waits for them, and re-layouts  33 us (23%)
  starting transfers between devices  17.3 us (12%)
  between operations  14.4 us (10%)
  matrix products  12.7 us (9%)
  other arithmetic  7.54 us (5%)
    all_gather x1, waiting for transfers between devices, body(): query_rows = (lax.all_gather(row_block, 'seq', axis=0, tiled=True),)[0]  35.1 us
    all_to_all x1, waiting for transfers between devices, body(): lax.all_to_all(computed[2], 'seq', split_axis=0, concat_axis=0, tiled=True)  24.3 us
    unnamed x27, local copies, waits for them, and re-layouts  11.6 us
    all_to_all x1, starting transfers between devices, body(): lax.all_to_all(computed[0], 'seq', split_axis=0, concat_axis=0, tiled=True)  6.03 us
    all_to_all x1, starting transfers between devices, body(): lax.all_to_all(computed[2], 'seq', split_axis=0, concat_axis=0, tiled=True)  6.02 us
    slice x1, local copies, waits for them, and re-layouts, body(): suffix_cache[:, :, :kv_width].reshape(cand_rows, suffix_len, kv_heads, HD)  5.57 us
    all_to_all x1, starting transfers between devices, body(): lax.all_to_all(computed[1], 'seq', split_axis=0, concat_axis=0, tiled=True)  5.19 us
    mul x2, local copies, waits for them, and re-layouts, body(): factor[..., None] * back_mix  4.05 us
  transfers between devices with their start and end apart: 4, of which 2 were waited for; matrix products, arithmetic and copies ran while one was open for 26% of the time, Pallas kernels for 0%

commit v1 on v0

v1 whole, which is shorter than its diff:
```python
import functools
import math

import jax
import jax.numpy as jnp
from jax import lax
from jax.experimental import pallas as pl
from jax.experimental.pallas import tpu as pltpu
from jax.sharding import PartitionSpec as P

HD = 128
BLOCK = 128
CORES = 2
FLOOR = -1e30
MESH = pl.DeviceIdType.MESH
F32 = jnp.float32
BF16 = jnp.bfloat16


def to_lanes(columns):
    rows = columns[0].shape[0]
    lane = lax.broadcasted_iota(jnp.int32, (rows, 128), 1)
    tile = jnp.zeros((rows, 128), F32)
    for index, column in enumerate(columns):
        tile = jnp.where(lane == index, column, tile)
    if rows < 128:
        tile = jnp.concatenate([tile, jnp.zeros((128 - rows, 128), F32)], axis=0)
    return jnp.transpose(tile)[:8]


def to_columns(lanes, rows):
    count = lanes.shape[0]
    tile = jnp.concatenate([lanes, jnp.zeros((128 - count, 128), F32)], axis=0)
    return jnp.transpose(tile)[:rows]


def kernel(
    sizes,
    q_ref,
    blocks_ref,
    weight_ref,
    prompt_hbm,
    suffix_hbm,
    out_ref,
    score_ref,
    kbuf,
    vbuf,
    sbuf,
    qbuf,
    own_mix,
    own_stat,
    y_mix,
    y_stat,
    y_mix_in,
    y_stat_in,
    z_mix,
    z_stat,
    z_mix_in,
    z_stat_in,
    suf_mix,
    suf_stat,
    kv_local,
    kv_send,
    kv_recv,
    suf_sem,
    qz_send,
    qz_recv,
    qy_send,
    qy_recv,
    ym_send,
    ym_recv,
    ys_send,
    ys_recv,
    zm_send,
    zm_recv,
    zs_send,
    zs_recv,
):
    A, B, cands, kv_heads, group = sizes
    half_heads = kv_heads // CORES
    piece = cands * group
    rows = half_heads * piece
    half_width = half_heads * HD
    kv_width = kv_heads * HD
    span = prompt_hbm.shape[1]
    prompts = prompt_hbm.shape[0]
    scale = HD**-0.5

    me = lax.axis_index("seq")
    c = lax.rem(me, CORES)
    y = lax.rem(me // CORES, B)
    z = me // (CORES * B)
    other = 1 - c

    def device(zz, yy, cc):
        return {"seq": (zz * B + yy) * CORES + cc}

    local = []
    for index, (buf, base) in enumerate(((kbuf, 0), (vbuf, kv_width))):
        copy = pltpu.make_async_copy(
            prompt_hbm.at[:, :, pl.ds(pl.multiple_of(base + c * half_width, 128), half_width)],
            buf.at[:, pl.ds(0, span), :],
            kv_local.at[index],
        )
        copy.start()
        local.append(copy)
    suffix_copies = []
    for cand in range(cands):
        copy = pltpu.make_async_copy(suffix_hbm.at[cand], sbuf.at[cand], suf_sem.at[cand])
        copy.start()
        suffix_copies.append(copy)

    barrier = pltpu.get_barrier_semaphore()
    pl.semaphore_signal(barrier, inc=1, device_id=device(z, y, other), device_id_type=MESH)
    for off in range(1, A):
        zz = lax.rem(z + off, A)
        for cc in range(CORES):
            pl.semaphore_signal(barrier, inc=1, device_id=device(zz, y, cc), device_id_type=MESH)
    for off in range(1, B):
        yy = lax.rem(y + off, B)
        pl.semaphore_signal(barrier, inc=1, device_id=device(z, yy, c), device_id_type=MESH)
    pl.semaphore_wait(barrier, 1 + CORES * (A - 1) + (B - 1))

    def q_copy(zz, cc, from_z, from_c):
        return pltpu.make_async_remote_copy(
            src_ref=q_ref.at[cc],
            dst_ref=qbuf.at[y, from_z, from_c],
            send_sem=qz_send.at[zz, cc],
            recv_sem=qz_recv.at[from_z, from_c],
            device_id=device(zz, y, cc),
            device_id_type=MESH,
        )

    q_copy(z, other, z, c).start()
    for off in range(1, A):
        zz = lax.rem(z + off, A)
        for cc in range(CORES):
            q_copy(zz, cc, z, c).start()
    qbuf[y, z, c] = q_ref[c]

    def kv_copy(index, buf, base):
        return pltpu.make_async_remote_copy(
            src_ref=prompt_hbm.at[
                :, :, pl.ds(pl.multiple_of(base + other * half_width, 128), half_width)
            ],
            dst_ref=buf.at[:, pl.ds(span, span), :],
            send_sem=kv_send.at[index],
            recv_sem=kv_recv.at[index],
            device_id=device(z, y, other),
            device_id_type=MESH,
        )

    kv_copies = [kv_copy(0, kbuf, 0), kv_copy(1, vbuf, kv_width)]
    for copy in kv_copies:
        copy.start()

    def y_copy(zz, yy, from_y):
        return pltpu.make_async_remote_copy(
            src_ref=qbuf.at[y, zz],
            dst_ref=qbuf.at[from_y, zz],
            send_sem=qy_send.at[yy, zz],
            recv_sem=qy_recv.at[from_y, zz],
            device_id=device(z, yy, c),
            device_id_type=MESH,
        )

    def forward(off):
        zz = lax.rem(z + off, A)
        if off == 0:
            q_copy(z, other, z, other).wait_recv()
        else:
            for cc in range(CORES):
                q_copy(zz, cc, zz, cc).wait_recv()
        for step in range(1, B):
            yy = lax.rem(y + step, B)
            y_copy(zz, yy, y).start()

    length = sbuf.shape[1]
    position = lax.broadcasted_iota(jnp.int32, (group, length), 1)

    def suffix(cand):
        suffix_copies[cand].wait()
        live = position < BLOCK * blocks_ref[cand]
        for head in range(kv_heads):
            side, inner = head // half_heads, head % half_heads
            start = inner * piece + cand * group
            query = q_ref[side].astype(F32)[start : start + group].astype(BF16)
            keys = sbuf[cand, :, head * HD : (head + 1) * HD]
            values = sbuf[cand, :, kv_width + head * HD : kv_width + (head + 1) * HD]
            logits = (
                lax.dot_general(query, keys, (((1,), (1,)), ((), ())), preferred_element_type=F32)
                * scale
            )
            logits = jnp.where(live, logits, FLOOR)
            top = jnp.max(logits, axis=1, keepdims=True)
            weights = jnp.where(live, jnp.exp(logits - top), 0.0)
            total = jnp.sum(weights, axis=1, keepdims=True)
            suf_mix[side, start : start + group, :] = jnp.dot(
                weights.astype(BF16), values, preferred_element_type=F32
            )
            suf_stat[side, 0, start : start + group, :] = jnp.broadcast_to(top, (group, 128))
            suf_stat[side, 1, start : start + group, :] = jnp.broadcast_to(total, (group, 128))

    forward(0)
    order = list(range(1, A))
    for cand in range(cands):
        suffix(cand)
        if cand < len(order):
            forward(order[cand])
    for off in order[cands:]:
        forward(off)

    for copy in local:
        copy.wait()
    for copy in kv_copies:
        copy.wait()

    def attend(yy, zz):
        packets = [qbuf[yy, zz, cc].astype(F32) for cc in range(CORES)]
        marks = jnp.concatenate(
            [
                jnp.broadcast_to(packets[cc][rows + cand : rows + cand + 1], (group, 128))
                for cc in range(CORES)
                for cand in range(cands)
            ],
            axis=0,
        )
        marks = jnp.concatenate([marks] * (CORES * span // 128), axis=1)
        tops, totals, mixes = [], [], []
        for head in range(half_heads):
            query = jnp.concatenate(
                [packets[cc][head * piece : (head + 1) * piece] for cc in range(CORES)], axis=0
            ).astype(BF16)
            lanes = slice(head * HD, (head + 1) * HD)
            logits = None
            for prompt in range(prompts):
                part = lax.dot_general(
                    query,
                    kbuf[prompt, :, lanes],
                    (((1,), (1,)), ((), ())),
                    preferred_element_type=F32,
                )
                logits = part if prompt == 0 else jnp.where(marks == prompt, part, logits)
            logits = logits * scale
            top = jnp.max(logits, axis=1, keepdims=True)
            weights = jnp.exp(logits - top)
            totals.append(jnp.sum(weights, axis=1, keepdims=True))
            tops.append(top)
            mix = None
            for prompt in range(prompts):
                part = jnp.dot(
                    jnp.where(marks == prompt, weights, 0.0).astype(BF16),
                    vbuf[prompt, :, lanes],
                    preferred_element_type=F32,
                )
                mix = part if mix is None else mix + part
            mixes.append(mix)

        def side(parts, cc):
            return jnp.concatenate([p[cc * piece : (cc + 1) * piece] for p in parts], axis=0)

        stat = to_lanes([side(tops, 0), side(tops, 1), side(totals, 0), side(totals, 1)])
        return stat, [side(mixes, cc) for cc in range(CORES)]

    def own(off, carry):
        zz = lax.rem(z + off, A)
        stat, mixes = attend(y, zz)
        own_stat[zz] = stat
        for cc in range(CORES):
            own_mix[zz, cc] = mixes[cc]
        return carry

    lax.fori_loop(0, A, own, 0)

    def ym_copy(zz, yy, from_y):
        return pltpu.make_async_remote_copy(
            src_ref=y_mix.at[yy, zz],
            dst_ref=y_mix_in.at[from_y, zz],
            send_sem=ym_send.at[yy, zz],
            recv_sem=ym_recv.at[from_y, zz],
            device_id=device(z, yy, c),
            device_id_type=MESH,
        )

    def ys_copy(zz, yy, from_y):
        return pltpu.make_async_remote_copy(
            src_ref=y_stat.at[yy, zz],
            dst_ref=y_stat_in.at[from_y, zz],
            send_sem=ys_send.at[yy, zz],
            recv_sem=ys_recv.at[from_y, zz],
            device_id=device(z, yy, c),
            device_id_type=MESH,
        )

    def helped(off, carry):
        zz = lax.rem(z + off, A)
        for step in range(1, B):
            yy = lax.rem(y + step, B)
            y_copy(zz, yy, yy).wait_recv()
            stat, mixes = attend(yy, zz)
            y_stat[yy, zz] = stat
            for cc in range(CORES):
                y_mix[yy, zz, cc] = mixes[cc].astype(BF16)
            ym_copy(zz, yy, y).start()
            ys_copy(zz, yy, y).start()
        return carry

    lax.fori_loop(0, A, helped, 0)

    def zm_copy(zz, cc, from_z, from_c):
        return pltpu.make_async_remote_copy(
            src_ref=z_mix.at[zz, cc],
            dst_ref=z_mix_in.at[from_z, from_c],
            send_sem=zm_send.at[zz, cc],
            recv_sem=zm_recv.at[from_z, from_c],
            device_id=device(zz, y, cc),
            device_id_type=MESH,
        )

    def zs_copy(zz, cc, from_z, from_c):
        return pltpu.make_async_remote_copy(
            src_ref=z_stat.at[zz, cc],
            dst_ref=z_stat_in.at[from_z, from_c],
            send_sem=zs_send.at[zz, cc],
            recv_sem=zs_recv.at[from_z, from_c],
            device_id=device(zz, y, cc),
            device_id_type=MESH,
        )

    def merged(zz):
        for step in range(1, B):
            yy = lax.rem(y + step, B)
            ym_copy(zz, yy, yy).wait_recv()
            ys_copy(zz, yy, yy).wait_recv()
        stats = [own_stat[zz]]
        for step in range(1, B):
            stats.append(y_stat_in[lax.rem(y + step, B), zz])
        top = functools.reduce(jnp.maximum, [s[0:2] for s in stats])
        factors = [jnp.exp(s[0:2] - top) for s in stats]
        total = sum(f * s[2:4] for f, s in zip(factors, stats))
        columns = to_columns(jnp.concatenate(factors, axis=0), rows)
        results = []
        for cc in range(CORES):
            mix = own_mix[zz, cc] * columns[:, cc : cc + 1]
            for step in range(1, B):
                arrived = y_mix_in[lax.rem(y + step, B), zz, cc].astype(F32)
                index = step * CORES + cc
                mix = mix + arrived * columns[:, index : index + 1]
            stat = jnp.concatenate(
                [top[cc : cc + 1], total[cc : cc + 1], jnp.zeros((6, 128), F32)], axis=0
            )
            results.append((mix.astype(BF16), stat))
        return results

    def returned(off, carry):
        zz = lax.rem(z + off, A)
        for cc, (mix, stat) in enumerate(merged(zz)):
            z_mix[zz, cc] = mix
            z_stat[zz, cc] = stat
            zm_copy(zz, cc, z, c).start()
            zs_copy(zz, cc, z, c).start()
        return carry

    lax.fori_loop(1, A, returned, 0)
    for cc, (mix, stat) in enumerate(merged(z)):
        z_mix[z, cc] = mix
        z_stat[z, cc] = stat
    zm_copy(z, other, z, c).start()
    zs_copy(z, other, z, c).start()
    z_mix_in[z, c] = z_mix[z, c]
    z_stat_in[z, c] = z_stat[z, c]

    zm_copy(z, other, z, other).wait_recv()
    zs_copy(z, other, z, other).wait_recv()
    for off in range(1, A):
        zz = lax.rem(z + off, A)
        for cc in range(CORES):
            zm_copy(zz, cc, zz, cc).wait_recv()
            zs_copy(zz, cc, zz, cc).wait_recv()

    scores = [0.0] * cands
    for side in range(CORES):
        suf = to_lanes([suf_stat[side, 0][:, 0:1], suf_stat[side, 1][:, 0:1]])
        stats = [z_stat_in[zz, side] for zz in range(A)] + [suf]
        top = functools.reduce(jnp.maximum, [s[0:1] for s in stats])
        factors = [jnp.exp(s[0:1] - top) for s in stats]
        total = sum(f * s[1:2] for f, s in zip(factors, stats))
        total = jnp.where(total > 0.0, total, 1.0)
        columns = to_columns(jnp.concatenate([f / total for f in factors], axis=0), rows)
        mix = suf_mix[side] * columns[:, A : A + 1]
        for zz in range(A):
            mix = mix + z_mix_in[zz, side].astype(F32) * columns[:, zz : zz + 1]
        half_rows = half_heads * group
        for cand in range(cands):
            picked = jnp.concatenate(
                [
                    mix[head * piece + cand * group : head * piece + (cand + 1) * group]
                    for head in range(half_heads)
                ],
                axis=0,
            ).astype(BF16)
            out_ref[cand, side * half_rows : (side + 1) * half_rows, :] = picked
            term = picked.astype(F32) * weight_ref[side * half_rows : (side + 1) * half_rows]
            scores[cand] = scores[cand] + jnp.sum(term)
    row = lax.broadcasted_iota(jnp.int32, (8, 128), 0)
    tile = jnp.zeros((8, 128), F32)
    for cand in range(cands):
        tile = jnp.where(row == cand, scores[cand], tile)
    score_ref[...] = tile

    q_copy(z, other, z, c).wait_send()
    zm_copy(z, other, z, c).wait_send()
    zs_copy(z, other, z, c).wait_send()

    def drain_z(off, carry):
        zz = lax.rem(z + off, A)
        for cc in range(CORES):
            q_copy(zz, cc, z, c).wait_send()
            zm_copy(zz, cc, z, c).wait_send()
            zs_copy(zz, cc, z, c).wait_send()
        return carry

    lax.fori_loop(1, A, drain_z, 0)

    def drain_y(zz, carry):
        for step in range(1, B):
            yy = lax.rem(y + step, B)
            y_copy(zz, yy, y).wait_send()
            ym_copy(zz, yy, y).wait_send()
            ys_copy(zz, yy, y).wait_send()
        return carry

    lax.fori_loop(0, A, drain_y, 0)


def body(A, B, queries, prompt_of, suffix_cache, suffix_blocks, prompt_cache, reward_weight):
    cands = queries.shape[0]
    heads = queries.shape[1] // HD
    prompts, span, width = prompt_cache.shape
    kv_heads = width // 2 // HD
    group = heads // kv_heads
    half_heads = kv_heads // CORES
    rows = half_heads * cands * group
    packet = rows + 16
    half_width = half_heads * HD

    ordered = queries.reshape(cands, CORES, half_heads, group, HD).transpose(1, 2, 0, 3, 4)
    ordered = ordered.reshape(CORES, rows, HD)
    marks = jnp.pad(prompt_of.astype(BF16), ((0, 16 - cands), (0, 0)))
    marks = jnp.broadcast_to(marks[None], (CORES, 16, HD))
    packed = jnp.concatenate([ordered, marks], axis=1)
    dma = pltpu.SemaphoreType.DMA

    attended, scores = pl.pallas_call(
        functools.partial(kernel, (A, B, cands, kv_heads, group)),
        out_shape=(
            jax.ShapeDtypeStruct((cands, heads, HD), BF16),
            jax.ShapeDtypeStruct((8, 128), F32),
        ),
        in_specs=[
            pl.BlockSpec(memory_space=pltpu.VMEM),
            pl.BlockSpec(memory_space=pltpu.SMEM),
            pl.BlockSpec(memory_space=pltpu.VMEM),
            pl.BlockSpec(memory_space=pl.ANY),
            pl.BlockSpec(memory_space=pl.ANY),
        ],
        out_specs=(
            pl.BlockSpec(memory_space=pltpu.VMEM),
            pl.BlockSpec(memory_space=pltpu.VMEM),
        ),
        scratch_shapes=[
            pltpu.VMEM((prompts, CORES * span, half_width), BF16),
            pltpu.VMEM((prompts, CORES * span, half_width), BF16),
            pltpu.VMEM(suffix_cache.shape, BF16),
            pltpu.VMEM((B, A, CORES, packet, HD), BF16),
            pltpu.VMEM((A, CORES, rows, HD), F32),
            pltpu.VMEM((A, 8, 128), F32),
            pltpu.VMEM((B, A, CORES, rows, HD), BF16),
            pltpu.VMEM((B, A, 8, 128), F32),
            pltpu.VMEM((B, A, CORES, rows, HD), BF16),
            pltpu.VMEM((B, A, 8, 128), F32),
            pltpu.VMEM((A, CORES, rows, HD), BF16),
            pltpu.VMEM((A, CORES, 8, 128), F32),
            pltpu.VMEM((A, CORES, rows, HD), BF16),
            pltpu.VMEM((A, CORES, 8, 128), F32),
            pltpu.VMEM((CORES, rows, HD), F32),
            pltpu.VMEM((CORES, 2, rows, 128), F32),
            dma((2,)),
            dma((2,)),
            dma((2,)),
            dma((cands,)),
            dma((A, CORES)),
            dma((A, CORES)),
            dma((B, A)),
            dma((B, A)),
            dma((B, A)),
            dma((B, A)),
            dma((B, A)),
            dma((B, A)),
            dma((A, CORES)),
            dma((A, CORES)),
            dma((A, CORES)),
            dma((A, CORES)),
        ],
        compiler_params=pltpu.CompilerParams(
            collective_id=0, has_side_effects=True, vmem_limit_bytes=48 * 1024 * 1024
        ),
    )(packed, suffix_blocks, reward_weight.reshape(heads, HD), prompt_cache, suffix_cache)
    return attended.reshape(cands, heads * HD), scores[:cands, 0]


def solution(mesh):
    chips = mesh.shape["seq"] // CORES
    B = 1
    while B * B * 4 <= chips and chips % (B * 2) == 0:
        B *= 2
    A = chips // B
    placed = (
        P(("groups", "seq"), None),
        P(("groups", "seq"), None),
        P(("groups", "seq"), None, None),
        P(("groups", "seq")),
        P("groups", "seq", None),
        P(),
    )
    return jax.shard_map(
        functools.partial(body, A, B),
        mesh=mesh,
        in_specs=placed,
        out_specs=(P(("groups", "seq"), None), P(("groups", "seq"))),
        check_vma=False,
    )
```

time: 145 us -> 40.9 us (0.28)
  the two profiles are of different devices: /device:TPU:13 before, /device:TPU:0 now
where the time goes in v1:
time: 40.9 us; the launch traced here: 40.7 us
  Pallas kernels  34.4 us (84%)
  local copies, waits for them, and re-layouts  4.88 us (12%)
  other arithmetic  0.74 us (2%)
  between operations  0.67 us (2%)
    pallas_call x1, Pallas kernels, body(): pl.pallas_call(functools.partial(kernel, (A, B, cands, kv_heads, group)),...  34.4 us
    unnamed x8, local copies, waits for them, and re-layouts  4.15 us

profile of v1, /device:TPU:0, one launch (start us, length us, event | category | flops | bytes accessed | tf_op | source)
XLA Modules:
  0.0 40.7 jit_solution(12597853480133241937)
XLA Ops:
  0.6 0.7 %convert_element_type.5 = bf16[3,1]{0,1:T(2,128)(2,1)S(1)} convert(s32[3,1]{0,1:T(1,128)} %param.7) | non-fusion elementwise | flops 3 | bytes 18 | tf_op jit(solution)/shard_map/convert_element_type | solution.py:449
  1.3 0.1 pad.6.clone
  1.4 0.8 %copy.10 = bf16[1,3,64,128]{3,2,1,0:T(8,128)(2,1)S(1)} copy(bf16[1,3,64,128]{3,1,2,0:T(4,128)(2,1)} %bitcast.17) | data formatting | bytes 98304
  2.2 0.1 pad_maximum_fusion.q_ref
  2.3 0.0 copy-start
  2.3 1.2 %copy-done = bf16[2,128,2048]{2,1,0:T(8,128)(2,1)S(1)} copy-done((bf16[2,128,2048]{2,1,0:T(8,128)(2,1)S(1)}, bf16[2,128,2048]{2,1,0:T(8,128)(2,1)}, u32[]{:S(2)}) %copy-start) | copy-done | bytes 1048600
  3.6 0.0 copy-start.1
  3.6 0.8 %copy-done.1 = f32[8192]{0:T(1024)S(1)} copy-done((f32[8192]{0:T(1024)S(1)}, f32[8192]{0:T(1024)}, u32[]{:S(2)}) %copy-start.1) | copy-done | bytes 32792
  4.3 0.0 copy-start.2
  4.3 0.7 %copy-done.2 = s32[3]{0:T(128)S(1)} copy-done((s32[3]{0:T(128)S(1)}, s32[3]{0:T(128)}, u32[]{:S(2)}) %copy-start.2) | copy-done | bytes 36
  5.0 34.4 %shard_map.77 = (bf16[3,64,128]{2,1,0:T(8,128)(2,1)S(1)}, f32[8,128]{1,0:T(8,128)S(1)}) custom-call(bf16[2,112,128]{2,1,0:T(8,128)(2,1)S(1)} %pad_maximum_fusion.q_ref, s32[3]{0:T(128)S(1)} %copy-done.2, f32[64,128]{1,0:T(8,128)S(1)} %bitcast.14, bf16[2,128,2048]{2,1,0:T(8,128)(2,1)S(1)} %copy-done, bf16[3,512,2048]{2,1,0:T(8,128)(2,1)} %suffix_hbm.1), custom_call_target="tpu_custom_call" | custom-call | tf_op jit(solution)/shard_map/pallas_call | solution.py:454
  39.4 0.6 %slice_reduce_fusion = f32[3]{0:T(128)} fusion(f32[8,128]{1,0:T(8,128)S(1)} %get-tuple-element.5), kind=kLoop, calls=%fused_computation.2 | loop fusion | bytes 24 | tf_op jit(solution)/shard_map/slice | solution.py:509
  40.0 0.7 %copy.13 = bf16[1,3,64,128]{3,1,2,0:T(4,128)(2,1)} copy(bf16[1,3,64,128]{3,2,1,0:T(8,128)(2,1)S(1)} %bitcast.13) | data formatting | bytes 98304
  (2 shorter events, 0.0 us)
Async XLA Ops:
  2.3 1.2 %copy-start = (bf16[2,128,2048]{2,1,0:T(8,128)(2,1)S(1)}, bf16[2,128,2048]{2,1,0:T(8,128)(2,1)}, u32[]{:S(2)}) copy-start(bf16[2,128,2048]{2,1,0:T(8,128)(2,1)} %prompt_hbm.1) | copy-start | bytes 3145732
  3.6 0.8 %copy-start.1 = (f32[8192]{0:T(1024)S(1)}, f32[8192]{0:T(1024)}, u32[]{:S(2)}) copy-start(f32[8192]{0:T(1024)} %param.11) | copy-start | bytes 98308
  4.3 0.7 %copy-start.2 = (s32[3]{0:T(128)S(1)}, s32[3]{0:T(128)}, u32[]{:S(2)}) copy-start(s32[3]{0:T(128)} %blocks_ref.1) | copy-start | bytes 40

commit v2 on v1

--- a/solution.py
+++ b/solution.py
@@ -36,13 +36,20 @@
 
 def kernel(
     sizes,
-    q_ref,
-    blocks_ref,
-    weight_ref,
+    q_hbm,
+    ids_hbm,
+    blocks_hbm,
+    weight_hbm,
     prompt_hbm,
     suffix_hbm,
     out_ref,
     score_ref,
+    q_raw,
+    q_ref,
+    ids_ref,
+    blocks_ref,
+    weight_ref,
+    small_sem,
     kbuf,
     vbuf,
     sbuf,
@@ -95,6 +102,18 @@
     def device(zz, yy, cc):
         return {"seq": (zz * B + yy) * CORES + cc}
 
+    small = []
+    for index, (src, dst) in enumerate(
+        (
+            (q_hbm, q_raw),
+            (ids_hbm, ids_ref),
+            (blocks_hbm, blocks_ref),
+            (weight_hbm, weight_ref),
+        )
+    ):
+        copy = pltpu.make_async_copy(src, dst, small_sem.at[index])
+        copy.start()
+        small.append(copy)
     local = []
     for index, (buf, base) in enumerate(((kbuf, 0), (vbuf, kv_width))):
         copy = pltpu.make_async_copy(
@@ -119,6 +138,24 @@
     for off in range(1, B):
         yy = lax.rem(y + off, B)
         pl.semaphore_signal(barrier, inc=1, device_id=device(z, yy, c), device_id_type=MESH)
+
+    small[0].wait()
+    small[1].wait()
+    raw = q_raw[...].astype(F32)
+    by_head = [raw[cand : cand + 1].reshape(kv_heads * group, HD) for cand in range(cands)]
+    row = lax.broadcasted_iota(jnp.int32, (16, HD), 0)
+    marked = jnp.zeros((16, HD), F32)
+    for cand in range(cands):
+        marked = jnp.where(row == cand, ids_ref[0, cand].astype(F32), marked)
+    for side in range(CORES):
+        pieces = [
+            by_head[cand][(side * half_heads + head) * group :][:group]
+            for head in range(half_heads)
+            for cand in range(cands)
+        ]
+        q_ref[side] = jnp.concatenate(pieces + [marked], axis=0).astype(BF16)
+    small[2].wait()
+    small[3].wait()
     pl.semaphore_wait(barrier, 1 + CORES * (A - 1) + (B - 1))
 
     def q_copy(zz, cc, from_z, from_c):
@@ -165,7 +202,7 @@
         )
 
     def forward(off):
-        zz = lax.rem(z + off, A)
+        zz = lax.rem(z - off + A, A)
         if off == 0:
             q_copy(z, other, z, other).wait_recv()
         else:
@@ -263,7 +300,7 @@
         return stat, [side(mixes, cc) for cc in range(CORES)]
 
     def own(off, carry):
-        zz = lax.rem(z + off, A)
+        zz = lax.rem(z - off + A, A)
         stat, mixes = attend(y, zz)
         own_stat[zz] = stat
         for cc in range(CORES):
@@ -293,7 +330,7 @@
         )
 
     def helped(off, carry):
-        zz = lax.rem(z + off, A)
+        zz = lax.rem(z - off + A, A)
         for step in range(1, B):
             yy = lax.rem(y + step, B)
             y_copy(zz, yy, yy).wait_recv()
@@ -353,7 +390,7 @@
         return results
 
     def returned(off, carry):
-        zz = lax.rem(z + off, A)
+        zz = lax.rem(z - off + A, A)
         for cc, (mix, stat) in enumerate(merged(zz)):
             z_mix[zz, cc] = mix
             z_stat[zz, cc] = stat
@@ -444,11 +481,6 @@
     packet = rows + 16
     half_width = half_heads * HD
 
-    ordered = queries.reshape(cands, CORES, half_heads, group, HD).transpose(1, 2, 0, 3, 4)
-    ordered = ordered.reshape(CORES, rows, HD)
-    marks = jnp.pad(prompt_of.astype(BF16), ((0, 16 - cands), (0, 0)))
-    marks = jnp.broadcast_to(marks[None], (CORES, 16, HD))
-    packed = jnp.concatenate([ordered, marks], axis=1)
     dma = pltpu.SemaphoreType.DMA
 
     attended, scores = pl.pallas_call(
@@ -458,17 +490,20 @@
             jax.ShapeDtypeStruct((8, 128), F32),
         ),
         in_specs=[
-            pl.BlockSpec(memory_space=pltpu.VMEM),
-            pl.BlockSpec(memory_space=pltpu.SMEM),
-            pl.BlockSpec(memory_space=pltpu.VMEM),
-            pl.BlockSpec(memory_space=pl.ANY),
-            pl.BlockSpec(memory_space=pl.ANY),
-        ],
+            pl.BlockSpec(memory_space=pltpu.HBM),
+        ]
+        * 6,
         out_specs=(
             pl.BlockSpec(memory_space=pltpu.VMEM),
             pl.BlockSpec(memory_space=pltpu.VMEM),
         ),
         scratch_shapes=[
+            pltpu.VMEM(queries.shape, BF16),
+            pltpu.VMEM((CORES, packet, HD), BF16),
+            pltpu.SMEM((1, cands), jnp.int32),
+            pltpu.SMEM(suffix_blocks.shape, jnp.int32),
+            pltpu.VMEM((heads, HD), F32),
+            dma((4,)),
             pltpu.VMEM((prompts, CORES * span, half_width), BF16),
             pltpu.VMEM((prompts, CORES * span, half_width), BF16),
             pltpu.VMEM(suffix_cache.shape, BF16),
@@ -503,9 +538,16 @@
             dma((A, CORES)),
         ],
         compiler_params=pltpu.CompilerParams(
-            collective_id=0, has_side_effects=True, vmem_limit_bytes=48 * 1024 * 1024
+            collective_id=0, has_side_effects=True, vmem_limit_bytes=63 * 1024 * 1024
         ),
-    )(packed, suffix_blocks, reward_weight.reshape(heads, HD), prompt_cache, suffix_cache)
+    )(
+        queries,
+        prompt_of.reshape(1, cands),
+        suffix_blocks,
+        reward_weight.reshape(heads, HD),
+        prompt_cache,
+        suffix_cache,
+    )
     return attended.reshape(cands, heads * HD), scores[:cands, 0]
 
 

time: 40.9 us -> 36.8 us (0.90)
  local copies, waits for them, and re-layouts: 4.88 us -> 2.78 us
  Pallas kernels: 34.4 us -> 33.2 us
  other arithmetic: 0.74 us -> 0 us
    unnamed x8 -> x1, local copies, waits for them, and re-layouts: 4.15 us -> 1.47 us
    pallas_call x1, Pallas kernels: 34.4 us -> 33.2 us  [body(): pl.pallas_call(functools.partial(kernel, (A, B, cands, kv_heads, group)),...]
    slice x1, local copies, waits for them, and re-layouts: 0.63 us -> 1.31 us  [body(): return (attended.reshape(cands, heads * HD), scores[:cands, 0])]
    convert_element_type x1 -> x0, other arithmetic: 0.66 us -> none  [body(): marks = jnp.pad(prompt_of.astype(BF16), ((0, 16 - cands), (0, 0)))]
where the time goes in v2:
time: 36.8 us; the launch traced here: 36.6 us
  Pallas kernels  33.2 us (90%)
  local copies, waits for them, and re-layouts  2.78 us (8%)
  between operations  0.64 us (2%)
    pallas_call x1, Pallas kernels, body(): pl.pallas_call(functools.partial(kernel, (A, B, cands, kv_heads, group)),...  33.2 us
    unnamed x1, local copies, waits for them, and re-layouts  1.47 us
    slice x1, local copies, waits for them, and re-layouts, body(): return (attended.reshape(cands, heads * HD), scores[:cands, 0])  1.31 us

profile of v2, /device:TPU:0, one launch (start us, length us, event | category | flops | bytes accessed | tf_op | source)
XLA Modules:
  0.0 36.6 jit_solution(1043328151990461463)
XLA Ops:
  0.6 33.2 %shard_map.77 = (bf16[3,64,128]{2,1,0:T(8,128)(2,1)}, f32[8,128]{1,0:T(8,128)}) custom-call(bf16[3,8192]{1,0:T(4,128)(2,1)} %q_hbm.1, s32[1,3]{1,0:T(1,128)} %bitcast.9, s32[3]{0:T(128)} %blocks_hbm.1, f32[64,128]{1,0:T(8,128)} %bitcast.8, bf16[2,128,2048]{2,1,0:T(8,128)(2,1)} %prompt_hbm.1, bf16[3,512,2048]{2,1,0:T(8,128)(2,1)} %suffix_hbm.1), custom_call_target="tpu_custom_call" | custom-call | tf_op jit(solution)/shard_map/pallas_call | solution.py:486
  33.8 1.3 %slice_reduce_fusion = f32[3]{0:T(128)} fusion(f32[8,128]{1,0:T(8,128)} %get-tuple-element.5), kind=kLoop, calls=%fused_computation.1 | loop fusion | bytes 24 | tf_op jit(solution)/shard_map/slice | solution.py:551
  35.1 1.5 %copy.10 = bf16[1,3,64,128]{3,1,2,0:T(4,128)(2,1)} copy(bf16[1,3,64,128]{3,2,1,0:T(8,128)(2,1)} %bitcast.7) | data formatting | bytes 98304

commit v3 on v2

--- a/solution.py
+++ b/solution.py
@@ -247,6 +247,9 @@
     for off in order[cands:]:
         forward(off)
 
+    suf_lanes = [
+        to_lanes([suf_stat[side, 0][:, 0:1], suf_stat[side, 1][:, 0:1]]) for side in range(CORES)
+    ]
     for copy in local:
         copy.wait()
     for copy in kv_copies:
@@ -299,15 +302,12 @@
         stat = to_lanes([side(tops, 0), side(tops, 1), side(totals, 0), side(totals, 1)])
         return stat, [side(mixes, cc) for cc in range(CORES)]
 
-    def own(off, carry):
+    def own(off):
         zz = lax.rem(z - off + A, A)
         stat, mixes = attend(y, zz)
         own_stat[zz] = stat
         for cc in range(CORES):
             own_mix[zz, cc] = mixes[cc]
-        return carry
-
-    lax.fori_loop(0, A, own, 0)
 
     def ym_copy(zz, yy, from_y):
         return pltpu.make_async_remote_copy(
@@ -329,7 +329,7 @@
             device_id_type=MESH,
         )
 
-    def helped(off, carry):
+    def helped(off):
         zz = lax.rem(z - off + A, A)
         for step in range(1, B):
             yy = lax.rem(y + step, B)
@@ -340,9 +340,6 @@
                 y_mix[yy, zz, cc] = mixes[cc].astype(BF16)
             ym_copy(zz, yy, y).start()
             ys_copy(zz, yy, y).start()
-        return carry
-
-    lax.fori_loop(0, A, helped, 0)
 
     def zm_copy(zz, cc, from_z, from_c):
         return pltpu.make_async_remote_copy(
@@ -389,16 +386,22 @@
             results.append((mix.astype(BF16), stat))
         return results
 
-    def returned(off, carry):
+    def returned(off):
         zz = lax.rem(z - off + A, A)
         for cc, (mix, stat) in enumerate(merged(zz)):
             z_mix[zz, cc] = mix
             z_stat[zz, cc] = stat
             zm_copy(zz, cc, z, c).start()
             zs_copy(zz, cc, z, c).start()
-        return carry
-
-    lax.fori_loop(1, A, returned, 0)
+
+    helped(0)
+    for off in range(1, A):
+        own(off)
+        helped(off)
+        if off >= 2:
+            returned(off - 1)
+    own(0)
+    returned(A - 1)
     for cc, (mix, stat) in enumerate(merged(z)):
         z_mix[z, cc] = mix
         z_stat[z, cc] = stat
@@ -417,8 +420,7 @@
 
     scores = [0.0] * cands
     for side in range(CORES):
-        suf = to_lanes([suf_stat[side, 0][:, 0:1], suf_stat[side, 1][:, 0:1]])
-        stats = [z_stat_in[zz, side] for zz in range(A)] + [suf]
+        stats = [z_stat_in[zz, side] for zz in range(A)] + [suf_lanes[side]]
         top = functools.reduce(jnp.maximum, [s[0:1] for s in stats])
         factors = [jnp.exp(s[0:1] - top) for s in stats]
         total = sum(f * s[1:2] for f, s in zip(factors, stats))

time: 36.8 us -> 35.3 us (0.959)
  Pallas kernels: 33.2 us -> 31.6 us
    pallas_call x1, Pallas kernels: 33.2 us -> 31.6 us  [body(): pl.pallas_call(functools.partial(kernel, (A, B, cands, kv_heads, group)),...]
where the time goes in v3:
time: 35.3 us; the launch traced here: 35.1 us
  Pallas kernels  31.6 us (90%)
  local copies, waits for them, and re-layouts  2.78 us (8%)
  between operations  0.64 us (2%)
    pallas_call x1, Pallas kernels, body(): pl.pallas_call(functools.partial(kernel, (A, B, cands, kv_heads, group)),...  31.6 us
    unnamed x1, local copies, waits for them, and re-layouts  1.47 us
    slice x1, local copies, waits for them, and re-layouts, body(): return (attended.reshape(cands, heads * HD), scores[:cands, 0])  1.31 us

profile of v3, /device:TPU:0, one launch (start us, length us, event | category | flops | bytes accessed | tf_op | source)
XLA Modules:
  0.0 35.1 jit_solution(12905722555569397523)
XLA Ops:
  0.6 31.6 %shard_map.77 = (bf16[3,64,128]{2,1,0:T(8,128)(2,1)}, f32[8,128]{1,0:T(8,128)}) custom-call(bf16[3,8192]{1,0:T(4,128)(2,1)} %q_hbm.1, s32[1,3]{1,0:T(1,128)} %bitcast.9, s32[3]{0:T(128)} %blocks_hbm.1, f32[64,128]{1,0:T(8,128)} %bitcast.8, bf16[2,128,2048]{2,1,0:T(8,128)(2,1)} %prompt_hbm.1, bf16[3,512,2048]{2,1,0:T(8,128)(2,1)} %suffix_hbm.1), custom_call_target="tpu_custom_call" | custom-call | tf_op jit(solution)/shard_map/pallas_call | solution.py:488
  32.3 1.3 %slice_reduce_fusion = f32[3]{0:T(128)} fusion(f32[8,128]{1,0:T(8,128)} %get-tuple-element.5), kind=kLoop, calls=%fused_computation.1 | loop fusion | bytes 24 | tf_op jit(solution)/shard_map/slice | solution.py:553
  33.6 1.5 %copy.10 = bf16[1,3,64,128]{3,1,2,0:T(4,128)(2,1)} copy(bf16[1,3,64,128]{3,2,1,0:T(8,128)(2,1)} %bitcast.7) | data formatting | bytes 98304

commit v4 on v3

--- a/solution.py
+++ b/solution.py
@@ -239,7 +239,7 @@
             suf_stat[side, 1, start : start + group, :] = jnp.broadcast_to(total, (group, 128))
 
     forward(0)
-    order = list(range(1, A))
+    order = list(range(1, A - 1))
     for cand in range(cands):
         suffix(cand)
         if cand < len(order):
@@ -395,6 +395,7 @@
             zs_copy(zz, cc, z, c).start()
 
     helped(0)
+    forward(A - 1)
     for off in range(1, A):
         own(off)
         helped(off)

time: 35.3 us -> 35.2 us (level)
  no operation moved by 1% of the time
where the time goes in v4:
time: 35.2 us; the launch traced here: 35 us
  Pallas kernels  31.6 us (90%)
  local copies, waits for them, and re-layouts  2.78 us (8%)
  between operations  0.64 us (2%)
    pallas_call x1, Pallas kernels, body(): pl.pallas_call(functools.partial(kernel, (A, B, cands, kv_heads, group)),...  31.6 us
    unnamed x1, local copies, waits for them, and re-layouts  1.47 us
    slice x1, local copies, waits for them, and re-layouts, body(): return (attended.reshape(cands, heads * HD), scores[:cands, 0])  1.31 us

profile of v4, /device:TPU:0, one launch (start us, length us, event | category | flops | bytes accessed | tf_op | source)
XLA Modules:
  0.0 35.0 jit_solution(7562473078798802022)
XLA Ops:
  0.6 31.6 %shard_map.77 = (bf16[3,64,128]{2,1,0:T(8,128)(2,1)}, f32[8,128]{1,0:T(8,128)}) custom-call(bf16[3,8192]{1,0:T(4,128)(2,1)} %q_hbm.1, s32[1,3]{1,0:T(1,128)} %bitcast.9, s32[3]{0:T(128)} %blocks_hbm.1, f32[64,128]{1,0:T(8,128)} %bitcast.8, bf16[2,128,2048]{2,1,0:T(8,128)(2,1)} %prompt_hbm.1, bf16[3,512,2048]{2,1,0:T(8,128)(2,1)} %suffix_hbm.1), custom_call_target="tpu_custom_call" | custom-call | tf_op jit(solution)/shard_map/pallas_call | solution.py:489
  32.2 1.3 %slice_reduce_fusion = f32[3]{0:T(128)} fusion(f32[8,128]{1,0:T(8,128)} %get-tuple-element.5), kind=kLoop, calls=%fused_computation.1 | loop fusion | bytes 24 | tf_op jit(solution)/shard_map/slice | solution.py:554
  33.5 1.5 %copy.10 = bf16[1,3,64,128]{3,1,2,0:T(4,128)(2,1)} copy(bf16[1,3,64,128]{3,2,1,0:T(8,128)(2,1)} %bitcast.7) | data formatting | bytes 98304
